TPU v7x, 32 devices: a whole 2x2x4 slice. The times are simulated.
32 devices in a mesh: flow: 8 (over y, x, core), cross: 4 (over z).
Axes of the slice: x: 2, y: 2, z: 4, core: 2. Of those that a mesh axis runs over, the one named last changes fastest.
Arguments:
- solid_temp: float32 [8, 2048, 2048], P(None, 'flow', 'cross'), may hold values from 0.5 to 1.5
- conductance: float32 [8, 2048, 2048], P(None, 'flow', 'cross'), may hold values from 0.03 to 0.12
- coolant: float32 [4, 2048, 2048], P(None, 'flow', 'cross'), may hold values from 0 to 1
- power_index: int32 [2048, 2048], P('flow', 'cross'), may hold values from 0 to 15
- power_levels: float32 [16], replicated, may hold values from 0.05 to 0.5
- channel_mask: int32 [4, 2048], P(None, 'cross'), may hold values 0 or 1
- inlet: float32 [4, 2048], P(None, 'cross'), may hold values from 0 to 0.5
- flow_gain: float32 [4, 2048], P(None, 'cross'), may hold values from 2 to 16
Outputs:
- solid_next: float32 [8, 2048, 2048], P(None, 'flow', 'cross')
- coolant_next: float32 [4, 2048, 2048], P(None, 'flow', 'cross')
All inputs are finite; a program needn't handle non-finite values. No bound on the sum of `channel_mask` on one device may be relied on, other than what follows from the above.
Results may differ from a plain program's by a relative error of at most 0.000058.
Values sent between devices are 32-bit elements; how exact they have to be, the bound alone decides.
A program may use at most 128 MiB of HBM per device.

v0:
```python
import jax
import jax.numpy as jnp
from jax import lax
from jax.sharding import PartitionSpec as P


def extended(shard, sides, width):
    for axis, dim in sides:
        size, length = (lax.axis_size(axis), shard.shape[dim])
        up = [(i, (i + 1) % size) for i in range(size - 1)]
        down = [(j, i) for i, j in up]
        last = lax.slice_in_dim(shard, length - width, length, axis=dim)
        initial = lax.slice_in_dim(shard, 0, width, axis=dim)
        before = lax.ppermute(last, axis, up)
        after = lax.ppermute(initial, axis, down)
        shard = jnp.concatenate([before, shard, after], axis=dim)
    return shard


def advance(padded, conduct, heating, coolant_now, open_cols):
    center = padded[:, 1:-1, 1:-1]
    lateral = (
        padded[:, 2:, 1:-1] + padded[:, :-2, 1:-1] + padded[:, 1:-1, 2:] + padded[:, 1:-1, :-2]
    )
    upward = center[1:] - center[:-1]
    no_layer = jnp.zeros_like(center[:1])
    vertical = jnp.concatenate([upward, no_layer], axis=0) - jnp.concatenate(
        [no_layer, upward], axis=0
    )
    chans = coolant_now.shape[0]
    paired = center.reshape(chans, 2, center.shape[1], center.shape[2])
    film_term = 0.08 * open_cols[:, None, None, :] * (coolant_now[:, None] - paired)
    source = jnp.concatenate([heating[None], jnp.zeros_like(center[1:])], axis=0)
    return (
        center
        + conduct * (lateral - 4.0 * center)
        + 0.05 * vertical
        + film_term.reshape(center.shape)
        + source
    )


def lookup_heat(power_index, power_levels):
    level_ids = jnp.arange(power_levels.shape[0], dtype=jnp.int32)
    matches = (power_index[None] == level_ids[:, None, None]).astype(jnp.float32)
    return jnp.sum(matches * power_levels[:, None, None], axis=0)


def shards(
    solid_temp, conductance, coolant, power_index, power_levels, channel_mask, inlet, flow_gain
):
    chans = coolant.shape[0]
    rows_dev = solid_temp.shape[1]
    cols_dev = solid_temp.shape[2]
    heating = lookup_heat(power_index, power_levels)
    open_cols = channel_mask.astype(jnp.float32)
    current = solid_temp
    for repeat in range(2):
        padded = extended(current, (("flow", 1), ("cross", 2)), 1)
        current = advance(padded, conductance, heating, coolant, open_cols)
    paired = current.reshape(chans, 2, rows_dev, cols_dev)
    absorbed = 0.08 * open_cols[:, None, :] * (paired[:, 0] + paired[:, 1] - 2.0 * coolant)
    row_pos = jnp.arange(rows_dev, dtype=jnp.int32)[:, None]
    col_pos = jnp.arange(rows_dev, dtype=jnp.int32)[None, :]
    triangle = jnp.where(col_pos < row_pos, 1.0, jnp.where(col_pos == row_pos, 0.5, 0.0)).astype(
        jnp.float32
    )
    within = jnp.einsum("ij,kjy->kiy", triangle, absorbed, precision=lax.Precision.HIGHEST)
    totals = jnp.sum(absorbed, axis=1)
    everyone = lax.all_gather(totals[None], "flow", axis=0, tiled=True)
    weights = (jnp.arange(everyone.shape[0], dtype=jnp.int32) < lax.axis_index("flow")).astype(
        jnp.float32
    )
    carried = jnp.sum(everyone * weights[:, None, None], axis=0)
    length_cells = float(rows_dev * lax.axis_size("flow"))
    fluid_new = (
        inlet[:, None, :] + flow_gain[:, None, :] * (carried[:, None, :] + within) / length_cells
    )
    return (current, fluid_new)


def solution(mesh):
    return jax.shard_map(
        shards,
        mesh=mesh,
        in_specs=(
            P(None, "flow", "cross"),
            P(None, "flow", "cross"),
            P(None, "flow", "cross"),
            P("flow", "cross"),
            P(),
            P(None, "cross"),
            P(None, "cross"),
            P(None, "cross"),
        ),
        out_specs=(P(None, "flow", "cross"), P(None, "flow", "cross")),
        check_vma=False,
    )
```

profile of v0, /device:TPU:0, one launch (start us, length us, event | category | flops | bytes accessed | tf_op | source)
XLA Modules:
  0.0 107.0 jit_solution(3209712518575930242)
XLA Ops:
  0.6 1.0 fusion.34
  1.6 1.3 %collective-permute-start = (f32[8,1,512]{2,1,0:T(1,128)S(1)}, f32[8,1,512]{2,1,0:T(1,128)S(1)}, u32[]{:S(2)}, u32[]{:S(2)}) collective-permute-start(f32[8,1,512]{2,1,0:T(1,128)S(1)} %get-tuple-element.19), channel_id=1, source_target_pairs={{4,0},{8,4},{12,8},{16,12},{20,16},{24,20},{28,24},{5,1},{9,5},{13... | collective-permute-start | bytes 49160 | tf_op jit(solution)/shard_map/ppermute | solution.py:15
  3.0 0.0 copy-start.1
  3.0 3.3 %collective-permute-start.1 = (f32[8,1,512]{2,1,0:T(1,128)S(1)}, f32[8,1,512]{2,1,0:T(1,128)S(1)}, u32[]{:S(2)}, u32[]{:S(2)}) collective-permute-start(f32[8,1,512]{2,1,0:T(1,128)S(1)} %get-tuple-element.18), channel_id=1, source_target_pairs={{0,4},{4,8},{8,12},{12,16},{16,20},{20,24},{24,28},{1,5},{5,9},{9,... | collective-permute-start | bytes 49160 | tf_op jit(solution)/shard_map/ppermute | solution.py:14
  6.3 5.9 %slice_subtract_fusion.1 = f32[7,256,512]{2,1,0:T(8,128)} fusion(f32[8,256,512]{2,1,0:T(8,128)} %param.8), kind=kLoop, calls=%fused_computation.41 | loop fusion | flops 917504 | bytes 11010048 | tf_op jit(solution)/shard_map/sub | solution.py:25
  12.2 0.9 select_reduce_fusion
  13.1 1.8 %pad_maximum_fusion.21 = (f32[8,258,1]{2,1,0:T(8,128)}, f32[8,258,1]{2,1,0:T(8,128)}) fusion(f32[8,1,512]{2,1,0:T(1,128)S(1)} %collective-permute-done, f32[8,256,512]{2,1,0:T(8,128)S(1)} %copy-done.1, f32[8,1,512]{2,1,0:T(1,128)S(1)} %collective-permute-done.1), kind=kLoop, calls=%fused_computation.54 | loop fusion | flops 8256 | bytes 4243584 | tf_op jit(solution)/shard_map/slice | solution.py:13
  14.9 1.7 %copy.45 = f32[8,258,1]{1,0,2:T(8,128)S(1)} copy(f32[8,258,1]{2,1,0:T(8,128)} %get-tuple-element.14) | data formatting | bytes 16512 | tf_op jit(solution)/shard_map/slice | solution.py:13
  16.6 1.3 %collective-permute-start.2 = (f32[8,258,1]{1,0,2:T(8,128)S(1)}, f32[8,258,1]{1,0,2:T(8,128)S(1)}, u32[]{:S(2)}, u32[]{:S(2)}) collective-permute-start(f32[8,258,1]{1,0,2:T(8,128)S(1)} %copy.45), channel_id=1, source_target_pairs={{1,0},{2,1},{3,2},{5,4},{6,5},{7,6},{9,8},{10,9},{11,10},{13,12},{... | collective-permute-start | bytes 24776 | tf_op jit(solution)/shard_map/ppermute | solution.py:15
  17.9 1.7 %copy.47 = f32[8,258,1]{1,0,2:T(8,128)S(1)} copy(f32[8,258,1]{2,1,0:T(8,128)} %get-tuple-element.15) | data formatting | bytes 16512 | tf_op jit(solution)/shard_map/slice | solution.py:12
  19.6 5.6 %collective-permute-start.3 = (f32[8,258,1]{1,0,2:T(8,128)S(1)}, f32[8,258,1]{1,0,2:T(8,128)S(1)}, u32[]{:S(2)}, u32[]{:S(2)}) collective-permute-start(f32[8,258,1]{1,0,2:T(8,128)S(1)} %copy.47), channel_id=1, source_target_pairs={{0,1},{1,2},{2,3},{4,5},{5,6},{6,7},{8,9},{9,10},{10,11},{12,13},{... | collective-permute-start | bytes 24776 | tf_op jit(solution)/shard_map/ppermute | solution.py:14
  25.2 1.4 %copy.46 = f32[8,258,1]{2,1,0:T(8,128)} copy(f32[8,258,1]{1,0,2:T(8,128)S(1)} %collective-permute-done.2) | data formatting | bytes 16512 | tf_op jit(solution)/shard_map/ppermute | solution.py:15
  26.6 1.4 %copy.48 = f32[8,258,1]{2,1,0:T(8,128)} copy(f32[8,258,1]{1,0,2:T(8,128)S(1)} %collective-permute-done.3) | data formatting | bytes 16512 | tf_op jit(solution)/shard_map/ppermute | solution.py:14
  28.0 15.3 %pad_add_fusion.1 = f32[8,256,512]{2,1,0:T(8,128)S(1)} fusion(f32[1,256,512]{2,1,0:T(8,128)S(1)} %bitcast.48, f32[8,256,512]{2,1,0:T(8,128)} %param.8, f32[8,256,512]{2,1,0:T(8,128)} %param.9, f32[8,258,1]{2,1,0:T(8,128)} %copy.48, f32[8,1,512]{2,1,0:T(1,128)S(1)} %collective-permute-done, f32[8,1,512]{2,1,0:T(1,128)S(1)} %collective-permute-done.1, ...), kind=kLoop, calls=%fused_computation.5 | loop fusion | flops 23068672 | bytes 18940032 | tf_op jit(solution)/shard_map/add | solution.py:35
  43.4 1.3 %collective-permute-start.4 = (f32[8,1,512]{2,1,0:T(1,128)S(1)}, f32[8,1,512]{2,1,0:T(1,128)S(1)}, u32[]{:S(2)}, u32[]{:S(2)}) collective-permute-start(f32[8,1,512]{2,1,0:T(1,128)S(1)} %get-tuple-element.17), channel_id=1, source_target_pairs={{4,0},{8,4},{12,8},{16,12},{20,16},{24,20},{28,24},{5,1},{9,5},{13... | collective-permute-start | bytes 49160 | tf_op jit(solution)/shard_map/ppermute | solution.py:15
  44.7 3.5 %collective-permute-start.5 = (f32[8,1,512]{2,1,0:T(1,128)S(1)}, f32[8,1,512]{2,1,0:T(1,128)S(1)}, u32[]{:S(2)}, u32[]{:S(2)}) collective-permute-start(f32[8,1,512]{2,1,0:T(1,128)S(1)} %get-tuple-element.16), channel_id=1, source_target_pairs={{0,4},{4,8},{8,12},{12,16},{16,20},{20,24},{24,28},{1,5},{5,9},{9,... | collective-permute-start | bytes 49160 | tf_op jit(solution)/shard_map/ppermute | solution.py:14
  48.3 0.8 collective-permute-done.5
  49.1 1.8 %pad_maximum_fusion.18 = (f32[8,258,1]{2,1,0:T(8,128)}, f32[8,258,1]{2,1,0:T(8,128)}) fusion(f32[8,1,512]{2,1,0:T(1,128)S(1)} %collective-permute-done.4, f32[8,256,512]{2,1,0:T(8,128)S(1)} %pad_add_fusion.1, f32[8,1,512]{2,1,0:T(1,128)S(1)} %collective-permute-done.5), kind=kLoop, calls=%fused_computation.51 | loop fusion | flops 8256 | bytes 4243584 | tf_op jit(solution)/shard_map/slice | solution.py:13
  50.8 1.7 %copy.49 = f32[8,258,1]{1,0,2:T(8,128)S(1)} copy(f32[8,258,1]{2,1,0:T(8,128)} %get-tuple-element.12) | data formatting | bytes 16512 | tf_op jit(solution)/shard_map/slice | solution.py:13
  52.5 1.3 %collective-permute-start.6 = (f32[8,258,1]{1,0,2:T(8,128)S(1)}, f32[8,258,1]{1,0,2:T(8,128)S(1)}, u32[]{:S(2)}, u32[]{:S(2)}) collective-permute-start(f32[8,258,1]{1,0,2:T(8,128)S(1)} %copy.49), channel_id=1, source_target_pairs={{1,0},{2,1},{3,2},{5,4},{6,5},{7,6},{9,8},{10,9},{11,10},{13,12},{... | collective-permute-start | bytes 24776 | tf_op jit(solution)/shard_map/ppermute | solution.py:15
  53.8 1.7 %copy.51 = f32[8,258,1]{1,0,2:T(8,128)S(1)} copy(f32[8,258,1]{2,1,0:T(8,128)} %get-tuple-element.13) | data formatting | bytes 16512 | tf_op jit(solution)/shard_map/slice | solution.py:12
  55.5 4.7 %collective-permute-start.7 = (f32[8,258,1]{1,0,2:T(8,128)S(1)}, f32[8,258,1]{1,0,2:T(8,128)S(1)}, u32[]{:S(2)}, u32[]{:S(2)}) collective-permute-start(f32[8,258,1]{1,0,2:T(8,128)S(1)} %copy.51), channel_id=1, source_target_pairs={{0,1},{1,2},{2,3},{4,5},{5,6},{6,7},{8,9},{9,10},{10,11},{12,13},{... | collective-permute-start | bytes 24776 | tf_op jit(solution)/shard_map/ppermute | solution.py:14
  60.3 5.8 %slice_subtract_fusion = f32[7,256,512]{2,1,0:T(8,128)} fusion(f32[8,256,512]{2,1,0:T(8,128)} %copy-done), kind=kLoop, calls=%fused_computation.40 | loop fusion | flops 917504 | bytes 11010048 | tf_op jit(solution)/shard_map/sub | solution.py:25
  66.1 1.4 %copy.50 = f32[8,258,1]{2,1,0:T(8,128)} copy(f32[8,258,1]{1,0,2:T(8,128)S(1)} %collective-permute-done.6) | data formatting | bytes 16512 | tf_op jit(solution)/shard_map/ppermute | solution.py:15
  67.5 1.4 %copy.52 = f32[8,258,1]{2,1,0:T(8,128)} copy(f32[8,258,1]{1,0,2:T(8,128)S(1)} %collective-permute-done.7) | data formatting | bytes 16512 | tf_op jit(solution)/shard_map/ppermute | solution.py:14
  68.9 15.6 %pad_add_fusion = f32[8,256,512]{2,1,0:T(8,128)S(1)} fusion(f32[1,256,512]{2,1,0:T(8,128)S(1)} %bitcast.49, f32[8,256,512]{2,1,0:T(8,128)} %copy-done, f32[8,256,512]{2,1,0:T(8,128)} %param.9, f32[8,258,1]{2,1,0:T(8,128)} %copy.52, f32[8,1,512]{2,1,0:T(1,128)S(1)} %collective-permute-done.4, f32[8,1,512]{2,1,0:T(1,128)S(1)} %collective-permute-done.5, ...), kind=kLoop, calls=%fused_computation.4 | loop fusion | flops 23068672 | bytes 18940032 | tf_op jit(solution)/shard_map/add | solution.py:35
  84.6 0.8 fusion.31
  85.4 1.2 %copy-done.3 = f32[8,256,512]{2,1,0:T(8,128)} copy-done((f32[8,256,512]{2,1,0:T(8,128)}, f32[8,256,512]{2,1,0:T(8,128)S(1)}, u32[]{:S(2)}) %copy-start.3) | copy-done | bytes 4194328
  86.5 14.3 %all-gather.1 = f32[8,4,512]{2,1,0:T(4,128)S(1)} all-gather(f32[1,4,512]{2,1,0:T(4,128)S(1)} %bitcast.50), channel_id=2, replica_groups=mesh['flow'=8,'cross'=4] {'flow'}, dimensions={0}, use_global_device_ids=true | all-gather | bytes 73728 | tf_op jit(solution)/shard_map/all_gather | solution.py:70
  100.9 0.1 multiply_reduce_fusion
  101.0 4.1 %add_bitcast_fusion = f32[4,256,512]{1,2,0:T(8,128)S(1)} fusion(f32[4,256,512]{2,1,0:T(8,128)S(1)} %get-tuple-element.11, f32[4,512]{1,0:T(4,128)S(1)} %multiply_reduce_fusion, f32[4,512]{1,0:T(4,128)S(1)} %copy-done.5, f32[4,512]{1,0:T(4,128)S(1)} %copy-done.6), kind=kOutput, calls=%fused_computation.48 | convolution fusion | flops 1612972032 | bytes 4218880 | tf_op jit(solution)/shard_map/ij,kjy->kiy/dot_general | solution.py:68
  105.1 1.8 %copy.56 = f32[4,256,512]{2,1,0:T(8,128)} copy(f32[4,256,512]{1,2,0:T(8,128)S(1)} %add_bitcast_fusion) | data formatting | bytes 4194304
  (28 shorter events, 0.1 us)
Async XLA Ops:
  1.6 11.5 %collective-permute-start = (f32[8,1,512]{2,1,0:T(1,128)S(1)}, f32[8,1,512]{2,1,0:T(1,128)S(1)}, u32[]{:S(2)}, u32[]{:S(2)}) collective-permute-start(f32[8,1,512]{2,1,0:T(1,128)S(1)} %get-tuple-element.19), channel_id=1, source_target_pairs={{4,0},{8,4},{12,8},{16,12},{20,16},{24,20},{28,24},{5,1},{9,5},{13... | collective-permute-start | bytes 49160 | tf_op jit(solution)/shard_map/ppermute | solution.py:15
  2.9 9.2 %copy-start.4 = (s32[256,512]{1,0:T(8,128)S(1)}, s32[256,512]{1,0:T(8,128)}, u32[]{:S(2)}) copy-start(s32[256,512]{1,0:T(8,128)} %param.11) | copy-start | bytes 1572868
  2.9 9.2 %copy-start.8 = (f32[16]{0:T(128)S(1)}, f32[16]{0:T(128)}, u32[]{:S(2)}) copy-start(f32[16]{0:T(128)} %param.12) | copy-start | bytes 196
  3.0 10.1 %copy-start.1 = (f32[8,256,512]{2,1,0:T(8,128)S(1)}, f32[8,256,512]{2,1,0:T(8,128)}, u32[]{:S(2)}) copy-start(f32[8,256,512]{2,1,0:T(8,128)} %param.8) | copy-start | bytes 12582916
  3.0 10.1 %collective-permute-start.1 = (f32[8,1,512]{2,1,0:T(1,128)S(1)}, f32[8,1,512]{2,1,0:T(1,128)S(1)}, u32[]{:S(2)}, u32[]{:S(2)}) collective-permute-start(f32[8,1,512]{2,1,0:T(1,128)S(1)} %get-tuple-element.18), channel_id=1, source_target_pairs={{0,4},{4,8},{8,12},{12,16},{16,20},{20,24},{24,28},{1,5},{5,9},{9,... | collective-permute-start | bytes 49160 | tf_op jit(solution)/shard_map/ppermute | solution.py:14
  13.1 12.1 %copy-start.7 = (s32[4,512]{1,0:T(4,128)S(1)}, s32[4,512]{1,0:T(4,128)}, u32[]{:S(2)}) copy-start(s32[4,512]{1,0:T(4,128)} %param.13) | copy-start | bytes 24580
  13.1 14.9 %copy-start.2 = (f32[4,256,512]{2,1,0:T(8,128)S(1)}, f32[4,256,512]{2,1,0:T(8,128)}, u32[]{:S(2)}) copy-start(f32[4,256,512]{2,1,0:T(8,128)} %param.10) | copy-start | bytes 6291460
  16.6 8.6 %collective-permute-start.2 = (f32[8,258,1]{1,0,2:T(8,128)S(1)}, f32[8,258,1]{1,0,2:T(8,128)S(1)}, u32[]{:S(2)}, u32[]{:S(2)}) collective-permute-start(f32[8,258,1]{1,0,2:T(8,128)S(1)} %copy.45), channel_id=1, source_target_pairs={{1,0},{2,1},{3,2},{5,4},{6,5},{7,6},{9,8},{10,9},{11,10},{13,12},{... | collective-permute-start | bytes 24776 | tf_op jit(solution)/shard_map/ppermute | solution.py:15
  19.6 7.0 %collective-permute-start.3 = (f32[8,258,1]{1,0,2:T(8,128)S(1)}, f32[8,258,1]{1,0,2:T(8,128)S(1)}, u32[]{:S(2)}, u32[]{:S(2)}) collective-permute-start(f32[8,258,1]{1,0,2:T(8,128)S(1)} %copy.47), channel_id=1, source_target_pairs={{0,1},{1,2},{2,3},{4,5},{5,6},{6,7},{8,9},{9,10},{10,11},{12,13},{... | collective-permute-start | bytes 24776 | tf_op jit(solution)/shard_map/ppermute | solution.py:14
  43.4 5.7 %copy-start = (f32[8,256,512]{2,1,0:T(8,128)}, f32[8,256,512]{2,1,0:T(8,128)S(1)}, u32[]{:S(2)}) copy-start(f32[8,256,512]{2,1,0:T(8,128)S(1)} %pad_add_fusion.1) | copy-start | bytes 12582916
  43.4 4.8 %collective-permute-start.4 = (f32[8,1,512]{2,1,0:T(1,128)S(1)}, f32[8,1,512]{2,1,0:T(1,128)S(1)}, u32[]{:S(2)}, u32[]{:S(2)}) collective-permute-start(f32[8,1,512]{2,1,0:T(1,128)S(1)} %get-tuple-element.17), channel_id=1, source_target_pairs={{4,0},{8,4},{12,8},{16,12},{20,16},{24,20},{28,24},{5,1},{9,5},{13... | collective-permute-start | bytes 49160 | tf_op jit(solution)/shard_map/ppermute | solution.py:15
  44.7 4.4 %collective-permute-start.5 = (f32[8,1,512]{2,1,0:T(1,128)S(1)}, f32[8,1,512]{2,1,0:T(1,128)S(1)}, u32[]{:S(2)}, u32[]{:S(2)}) collective-permute-start(f32[8,1,512]{2,1,0:T(1,128)S(1)} %get-tuple-element.16), channel_id=1, source_target_pairs={{0,4},{4,8},{8,12},{12,16},{16,20},{20,24},{24,28},{1,5},{5,9},{9,... | collective-permute-start | bytes 49160 | tf_op jit(solution)/shard_map/ppermute | solution.py:14
  52.5 13.6 %collective-permute-start.6 = (f32[8,258,1]{1,0,2:T(8,128)S(1)}, f32[8,258,1]{1,0,2:T(8,128)S(1)}, u32[]{:S(2)}, u32[]{:S(2)}) collective-permute-start(f32[8,258,1]{1,0,2:T(8,128)S(1)} %copy.49), channel_id=1, source_target_pairs={{1,0},{2,1},{3,2},{5,4},{6,5},{7,6},{9,8},{10,9},{11,10},{13,12},{... | collective-permute-start | bytes 24776 | tf_op jit(solution)/shard_map/ppermute | solution.py:15
  55.5 12.0 %collective-permute-start.7 = (f32[8,258,1]{1,0,2:T(8,128)S(1)}, f32[8,258,1]{1,0,2:T(8,128)S(1)}, u32[]{:S(2)}, u32[]{:S(2)}) collective-permute-start(f32[8,258,1]{1,0,2:T(8,128)S(1)} %copy.51), channel_id=1, source_target_pairs={{0,1},{1,2},{2,3},{4,5},{5,6},{6,7},{8,9},{9,10},{10,11},{12,13},{... | collective-permute-start | bytes 24776 | tf_op jit(solution)/shard_map/ppermute | solution.py:14
  84.5 2.0 %copy-start.3 = (f32[8,256,512]{2,1,0:T(8,128)}, f32[8,256,512]{2,1,0:T(8,128)S(1)}, u32[]{:S(2)}) copy-start(f32[8,256,512]{2,1,0:T(8,128)S(1)} %pad_add_fusion) | copy-start | bytes 12582916
  84.5 16.4 %copy-start.5 = (f32[4,512]{1,0:T(4,128)S(1)}, f32[4,512]{1,0:T(4,128)}, u32[]{:S(2)}) copy-start(f32[4,512]{1,0:T(4,128)} %param.15) | copy-start | bytes 24580
  84.6 16.4 %copy-start.6 = (f32[4,512]{1,0:T(4,128)S(1)}, f32[4,512]{1,0:T(4,128)}, u32[]{:S(2)}) copy-start(f32[4,512]{1,0:T(4,128)} %param.14) | copy-start | bytes 24580
where the time goes:
time: 107 us
  other arithmetic  48 us (45%)
  starting transfers between devices  22.3 us (21%)
  local copies, waits for them, and re-layouts  16.5 us (15%)
  blocking collectives  14.3 us (13%)
  matrix products  4.14 us (4%)
    add x2, other arithmetic, advance(): center + conduct * (lateral - 4.0 * center) + 0.05 * vertical  30.9 us
    ppermute x4, starting transfers between devices, extended(): before = lax.ppermute(last, axis, up)  17.1 us
    all_gather x1, blocking collectives, shards(): everyone = lax.all_gather(totals[None], 'flow', axis=0, tiled=True)  14.3 us
    sub x2, other arithmetic, advance(): upward = center[1:] - center[:-1]  11.7 us
    ppermute x4, starting transfers between devices, extended(): after = lax.ppermute(initial, axis, down)  5.17 us
    slice x4, local copies, waits for them, and re-layouts, extended(): last = lax.slice_in_dim(shard, length - width, length, axis=dim)  4.44 us
    dot_general x1, matrix products, shards(): jnp.einsum('ij,kjy->kiy', triangle, absorbed, precision=lax.Precision.HIG...  4.14 us
    slice x2, other arithmetic, extended(): initial = lax.slice_in_dim(shard, 0, width, axis=dim)  3.53 us
  transfers between devices with their start and end apart: 8, of which 1 were waited for; matrix products, arithmetic and copies ran while one was open for 18% of the time, Pallas kernels for 0%

commit v1 on v0

v1 whole, which is shorter than its diff:
```python
import functools

import jax
import jax.numpy as jnp
from jax import lax
from jax.experimental import pallas as pl
from jax.experimental.pallas import tpu as pltpu
from jax.sharding import PartitionSpec as P

MESH = pl.DeviceIdType.MESH
LANES = 128
CHUNK = 16


def stencil(src, layer, start, size):
    width = src.shape[2]
    block = src[layer, pl.ds(start, size + 16), :]
    center = block[8 : size + 8]
    above = pltpu.roll(block, 1, 0)[8 : size + 8]
    below = pltpu.roll(block, size + 15, 0)[8 : size + 8]
    lane = lax.broadcasted_iota(jnp.int32, (size, LANES), 1)
    tiles = [center[:, j : j + LANES] for j in range(0, width, LANES)]
    none = jnp.zeros((size, LANES), jnp.float32)
    right_by_one = [none] + [pltpu.roll(t, 1, 1) for t in tiles]
    left_by_one = [pltpu.roll(t, LANES - 1, 1) for t in tiles] + [none]
    sides = []
    for j in range(len(tiles)):
        left = jnp.where(lane == 0, right_by_one[j], right_by_one[j + 1])
        right = jnp.where(lane == LANES - 1, left_by_one[j + 1], left_by_one[j])
        sides.append(left + right)
    return center, above + below + jnp.concatenate(sides, axis=1)


def advance(src, cond, cool, film, heat, start, size, store):
    layers = src.shape[0]
    parts = [stencil(src, l, start, size) for l in range(layers)]
    rows = pl.ds(start, size)
    for l in range(layers):
        k = l // 2
        u, lateral = parts[l]
        near = [parts[m][0] for m in (l - 1, l + 1) if 0 <= m < layers]
        keep = (1.0 - 0.05 * len(near)) - film[k : k + 1, :]
        new = u * keep + cond[l, rows, :] * (lateral - 4.0 * u)
        new = new + 0.05 * (near[0] + near[1] if len(near) == 2 else near[0])
        new = new + film[k : k + 1, :] * cool[k, rows, :]
        if l == 0:
            new = new + heat
        store(l, new)


def pick(index, levels, count):
    values = [levels[i] for i in range(count)]
    bit = 1
    while len(values) > 1:
        if len(values) % 2:
            values.append(values[-1])
        odd = (index & bit) != 0
        values = [jnp.where(odd, values[i + 1], values[i]) for i in range(0, len(values), 2)]
        bit *= 2
    return values[0]


def kernel(
    n_flow, n_cross,
    u_hbm, c_hbm, cool_hbm, idx_hbm, lev_hbm, mask_hbm, inlet_hbm, gain_hbm,
    out, fluid,
    u0, u1, cond, cool, idx, heat, abs_hi, abs_lo, lev, mask, inlet, gain,
    row_out, col_out, row_in, col_in, tot_out, tot_in,
    big_sem, small_sem, halo_send, halo_recv, tot_send, tot_recv,
):
    layers, rows, width = u_hbm.shape
    chans = cool_hbm.shape[0]
    blocks = rows // 8
    per = LANES // layers
    groups = 4 if rows % (4 * CHUNK) == 0 else 1
    span = rows // groups
    me_f, me_c = lax.axis_index("flow"), lax.axis_index("cross")

    def loads(g):
        part = pl.ds(g * span, span)
        return [
            pltpu.make_async_copy(c_hbm.at[:, part], cond.at[:, part], big_sem.at[g, 1]),
            pltpu.make_async_copy(cool_hbm.at[:, part], cool.at[:, part], big_sem.at[g, 2]),
            pltpu.make_async_copy(idx_hbm.at[part], idx.at[part], big_sem.at[g, 3]),
        ]

    def load_u(g):
        return pltpu.make_async_copy(
            u_hbm.at[:, pl.ds(g * span, span)],
            u0.at[:, pl.ds(8 + g * span, span)],
            big_sem.at[g, 0],
        )

    small = [
        pltpu.make_async_copy(src, dst, small_sem.at[i])
        for i, (src, dst) in enumerate(
            [(lev_hbm, lev), (mask_hbm, mask), (inlet_hbm, inlet), (gain_hbm, gain)]
        )
    ]
    for g in range(groups):
        load_u(g).start()
    for s in small:
        s.start()
    for g in range(groups):
        for one in loads(g):
            one.start()

    barrier = pltpu.get_barrier_semaphore()
    for d in range(1, n_flow):
        pl.semaphore_signal(
            barrier, inc=1, device_id=(lax.rem(me_f + d, n_flow), me_c), device_id_type=MESH
        )

    @pl.when(me_c > 0)
    def _():
        pl.semaphore_signal(barrier, inc=1, device_id=(me_f, me_c - 1), device_id_type=MESH)

    @pl.when(me_c < n_cross - 1)
    def _():
        pl.semaphore_signal(barrier, inc=1, device_id=(me_f, me_c + 1), device_id_type=MESH)

    zeros = jnp.zeros((layers, 8, width), jnp.float32)
    for ref in (u0, u1):
        ref[:, 0:8, :] = zeros
        ref[:, rows + 8 : rows + 16, :] = zeros
    col_out[...] = jnp.zeros_like(col_out)
    tot_out[...] = jnp.zeros_like(tot_out)

    has = [me_f > 0, me_f < n_flow - 1, me_c > 0, me_c < n_cross - 1]
    peer = [
        (jnp.maximum(me_f - 1, 0), me_c),
        (jnp.minimum(me_f + 1, n_flow - 1), me_c),
        (me_f, jnp.maximum(me_c - 1, 0)),
        (me_f, jnp.minimum(me_c + 1, n_cross - 1)),
    ]

    def halo(turn, d):
        send, recv = (row_out, row_in) if d < 2 else (col_out, col_in)
        return pltpu.make_async_remote_copy(
            src_ref=send.at[turn, d % 2],
            dst_ref=recv.at[turn, 1 - d % 2],
            send_sem=halo_send.at[turn, d],
            recv_sem=halo_recv.at[turn, d + 1 - 2 * (d % 2)],
            device_id=peer[d],
            device_id_type=MESH,
        )

    def arrival(turn, d):
        recv = row_in if d < 2 else col_in
        return pltpu.make_async_remote_copy(
            src_ref=recv.at[turn, d % 2],
            dst_ref=recv.at[turn, d % 2],
            send_sem=halo_send.at[turn, d],
            recv_sem=halo_recv.at[turn, d],
            device_id=peer[d],
            device_id_type=MESH,
        )

    def send_halos(turn):
        for d in (2, 3, 0, 1):
            @pl.when(has[d])
            def _():
                halo(turn, d).start()

    def take_halos(turn):
        for d in range(4):
            @pl.when(has[d])
            def _():
                arrival(turn, d).wait_recv()

            @pl.when(jnp.logical_not(has[d]))
            def _():
                recv = row_in if d < 2 else col_in
                recv[turn, d % 2] = jnp.zeros(recv.shape[2:], jnp.float32)

    lane = lax.broadcasted_iota(jnp.int32, (8, LANES), 1)

    def pack_cols(turn, b, lefts, rights):
        base = lax.rem(b, per) * layers
        where = pl.ds(pl.multiple_of((b // per) * 8, 8), 8)
        for side, tiles in enumerate((lefts, rights)):
            joined = jnp.zeros((8, LANES), jnp.float32)
            for l, tile in enumerate(tiles):
                shift = (l + side) % LANES
                moved = pltpu.roll(tile, shift, 1) if shift else tile
                joined = jnp.where(lane == l, moved, joined)
            joined = pltpu.roll(joined, base, 1)
            mine = (lane >= base) & (lane < base + layers)
            col_out[turn, side, where, :] = jnp.where(mine, joined, col_out[turn, side, where, :])

    def fix_cols(turn, b, ref, pad):
        base = lax.rem(b, per) * layers
        where = pl.ds(pl.multiple_of((b // per) * 8, 8), 8)
        at = pl.multiple_of(b * 8, 8)
        edges = []
        for side in range(2):
            cols = pl.ds(0, LANES) if side == 0 else pl.ds(width - LANES, LANES)
            target = 0 if side == 0 else LANES - 1
            packed = pltpu.roll(col_in[turn, side, where, :], lax.rem(LANES - base, LANES), 1)
            tiles = []
            for l in range(layers):
                shift = (target - l) % LANES
                beyond = pltpu.roll(packed, shift, 1) if shift else packed
                term = jnp.where(lane == target, beyond * cond[l, pl.ds(at, 8), cols], 0.0)
                tile = ref[l, pl.ds(at + pad, 8), cols] + term
                ref[l, pl.ds(at + pad, 8), cols] = tile
                tiles.append(tile)
            edges.append(tiles)
        return edges

    def fix_rows(turn, ref, pad):
        for l in range(layers):
            for side, row in ((0, 0), (1, rows - 1)):
                at = pl.ds(pad + row, 1)
                ref[l, at, :] = (
                    ref[l, at, :] + cond[l, pl.ds(row, 1), :] * row_in[turn, side, pl.ds(l, 1), :]
                )

    def pack_rows(turn, ref):
        for l in range(layers):
            row_out[turn, 0, pl.ds(l, 1), :] = ref[l, pl.ds(8, 1), :]
            row_out[turn, 1, pl.ds(l, 1), :] = ref[l, pl.ds(rows + 7, 1), :]

    per_group = blocks // groups
    for g in range(groups):
        load_u(g).wait()

        def pack(i, _):
            b = g * per_group + i
            at = pl.ds(pl.multiple_of(b * 8 + 8, 8), 8)
            pack_cols(
                0, b,
                [u0[l, at, pl.ds(0, LANES)] for l in range(layers)],
                [u0[l, at, pl.ds(width - LANES, LANES)] for l in range(layers)],
            )
            return 0

        lax.fori_loop(0, per_group, pack, 0)
    pack_rows(0, u0)
    pl.semaphore_wait(barrier, n_flow - 1 + has[2].astype(jnp.int32) + has[3].astype(jnp.int32))
    send_halos(0)

    for s in small:
        s.wait()
    film = 0.08 * mask[...].astype(jnp.float32)

    for g in range(groups):
        for one in loads(g):
            one.wait()

        def first(i, _):
            start = pl.multiple_of(g * span + i * CHUNK, CHUNK)
            warm = pick(idx[pl.ds(start, CHUNK), :], lev, lev.shape[0])
            heat[pl.ds(start, CHUNK), :] = warm

            def store(l, new):
                u1[l, pl.ds(start + 8, CHUNK), :] = new

            advance(u0, cond, cool, film, warm, start, CHUNK, store)
            return 0

        lax.fori_loop(0, span // CHUNK, first, 0)

    take_halos(0)
    fix_rows(0, u1, 8)

    def fix_first(b, _):
        lefts, rights = fix_cols(0, b, u1, 8)
        pack_cols(1, b, lefts, rights)
        return 0

    lax.fori_loop(0, blocks, fix_first, 0)
    pack_rows(1, u1)
    send_halos(1)

    def second(i, _):
        start = pl.multiple_of(i * CHUNK, CHUNK)

        def store(l, new):
            out[l, pl.ds(start, CHUNK), :] = new

        advance(u1, cond, cool, film, heat[pl.ds(start, CHUNK), :], start, CHUNK, store)
        return 0

    lax.fori_loop(0, rows // CHUNK, second, 0)
    take_halos(1)
    fix_rows(1, out, 0)

    def fix_second(b, _):
        fix_cols(1, b, out, 0)
        return 0

    lax.fori_loop(0, blocks, fix_second, 0)

    def take_up(i, sums):
        at = pl.ds(pl.multiple_of(i * CHUNK, CHUNK), CHUNK)
        new = []
        for k in range(chans):
            taken = film[k : k + 1, :] * (
                out[2 * k, at, :] + out[2 * k + 1, at, :] - 2.0 * cool[k, at, :]
            )
            high = taken.astype(jnp.bfloat16)
            abs_hi[k, at, :] = high
            abs_lo[k, at, :] = (taken - high.astype(jnp.float32)).astype(jnp.bfloat16)
            total = sums[k]
            for s in range(0, CHUNK, 8):
                total = total + taken[s : s + 8]
            new.append(total)
        return tuple(new)

    sums = lax.fori_loop(
        0, rows // CHUNK, take_up,
        tuple(jnp.zeros((8, width), jnp.float32) for _ in range(chans)),
    )
    for k in range(chans):
        tot_out[pl.ds(k, 1), :] = jnp.sum(sums[k], axis=0, keepdims=True)

    def carry(d):
        return pltpu.make_async_remote_copy(
            src_ref=tot_out,
            dst_ref=tot_in.at[d - 1],
            send_sem=tot_send.at[d - 1],
            recv_sem=tot_recv.at[d - 1],
            device_id=(lax.rem(me_f + d, n_flow), me_c),
            device_id_type=MESH,
        )

    for d in range(1, n_flow):
        @pl.when(me_f + d < n_flow)
        def _():
            carry(d).start()

    i_pos = lax.broadcasted_iota(jnp.int32, (rows, rows), 0)
    j_pos = lax.broadcasted_iota(jnp.int32, (rows, rows), 1)
    triangle = jnp.where(j_pos < i_pos, 1.0, jnp.where(j_pos == i_pos, 0.5, 0.0)).astype(
        jnp.bfloat16
    )
    for k in range(chans):
        fluid[k] = jnp.dot(
            triangle, abs_hi[k], preferred_element_type=jnp.float32
        ) + jnp.dot(triangle, abs_lo[k], preferred_element_type=jnp.float32)

    for d in range(1, n_flow):
        @pl.when(me_f >= d)
        def _():
            carry(d).wait_recv()

        @pl.when(me_f < d)
        def _():
            tot_in[d - 1] = jnp.zeros(tot_in.shape[1:], jnp.float32)

    carried = tot_in[0]
    for d in range(2, n_flow):
        carried = carried + tot_in[d - 1]
    scale = gain[...] * (1.0 / (rows * n_flow))
    origin = inlet[...] + scale * carried[:chans]

    def march(i, _):
        at = pl.ds(pl.multiple_of(i * CHUNK, CHUNK), CHUNK)
        for k in range(chans):
            fluid[k, at, :] = origin[k : k + 1, :] + scale[k : k + 1, :] * fluid[k, at, :]
        return 0

    lax.fori_loop(0, rows // CHUNK, march, 0)

    for turn in range(2):
        for d in range(4):
            @pl.when(has[d])
            def _():
                halo(turn, d).wait_send()
    for d in range(1, n_flow):
        @pl.when(me_f + d < n_flow)
        def _():
            carry(d).wait_send()


def shards(
    solid_temp, conductance, coolant, power_index, power_levels, channel_mask, inlet, flow_gain
):
    n_flow, n_cross = lax.axis_size("flow"), lax.axis_size("cross")
    layers, rows, width = solid_temp.shape
    chans = coolant.shape[0]
    f32 = jnp.float32
    packed = pl.cdiv(rows // 8, LANES // layers) * 8
    totals = pl.cdiv(chans, 8) * 8
    scratch = [
        pltpu.VMEM((layers, rows + 16, width), f32),
        pltpu.VMEM((layers, rows + 16, width), f32),
        pltpu.VMEM((layers, rows, width), f32),
        pltpu.VMEM((chans, rows, width), f32),
        pltpu.VMEM((rows, width), jnp.int32),
        pltpu.VMEM((rows, width), f32),
        pltpu.VMEM((chans, rows, width), jnp.bfloat16),
        pltpu.VMEM((chans, rows, width), jnp.bfloat16),
        pltpu.SMEM(power_levels.shape, f32),
        pltpu.VMEM((chans, width), jnp.int32),
        pltpu.VMEM((chans, width), f32),
        pltpu.VMEM((chans, width), f32),
        pltpu.VMEM((2, 2, layers, width), f32),
        pltpu.VMEM((2, 2, packed, LANES), f32),
        pltpu.VMEM((2, 2, layers, width), f32),
        pltpu.VMEM((2, 2, packed, LANES), f32),
        pltpu.VMEM((totals, width), f32),
        pltpu.VMEM((n_flow - 1, totals, width), f32),
        pltpu.SemaphoreType.DMA((4, 4)),
        pltpu.SemaphoreType.DMA((4,)),
        pltpu.SemaphoreType.DMA((2, 4)),
        pltpu.SemaphoreType.DMA((2, 4)),
        pltpu.SemaphoreType.DMA((n_flow - 1,)),
        pltpu.SemaphoreType.DMA((n_flow - 1,)),
    ]
    cells = layers * rows * width
    return pl.pallas_call(
        functools.partial(kernel, n_flow, n_cross),
        out_shape=(
            pltpu.VMEM((layers, rows, width), f32),
            pltpu.VMEM((chans, rows, width), f32),
        ),
        in_specs=[pl.BlockSpec(memory_space=pltpu.HBM)] * 8,
        out_specs=(
            pl.BlockSpec(memory_space=pltpu.VMEM),
            pl.BlockSpec(memory_space=pltpu.VMEM),
        ),
        scratch_shapes=scratch,
        compiler_params=pltpu.CompilerParams(
            collective_id=0, has_side_effects=True, vmem_limit_bytes=57 * 1024 * 1024
        ),
        cost_estimate=pl.CostEstimate(
            flops=40 * cells, bytes_accessed=17 * cells, transcendentals=0
        ),
    )(
        solid_temp, conductance, coolant, power_index, power_levels, channel_mask, inlet, flow_gain
    )


def solution(mesh):
    return jax.shard_map(
        shards,
        mesh=mesh,
        in_specs=(
            P(None, "flow", "cross"),
            P(None, "flow", "cross"),
            P(None, "flow", "cross"),
            P("flow", "cross"),
            P(),
            P(None, "cross"),
            P(None, "cross"),
            P(None, "cross"),
        ),
        out_specs=(P(None, "flow", "cross"), P(None, "flow", "cross")),
        check_vma=False,
    )
```

time: 107 us -> 36.9 us (0.34)
  the two profiles are of different devices: /device:TPU:0 before, /device:TPU:13 now
where the time goes in v1:
time: 36.9 us; the launch traced here: 36.8 us
  Pallas kernels  32.8 us (89%)
  local copies, waits for them, and re-layouts  3.33 us (9%)
  between operations  0.64 us (2%)
    pallas_call x1, Pallas kernels, shards(): pl.pallas_call(functools.partial(kernel, n_flow, n_cross), out_shape=(plt...  32.8 us
    unnamed x2, local copies, waits for them, and re-layouts  3.33 us

profile of v1, /device:TPU:13, one launch (start us, length us, event | category | flops | bytes accessed | tf_op | source)
XLA Modules:
  0.0 36.8 jit_solution(3096368944521954886)
XLA Ops:
  0.6 32.8 %shard_map.95 = (f32[8,256,512]{2,1,0:T(8,128)S(1)}, f32[4,256,512]{2,1,0:T(8,128)S(1)}) custom-call(f32[8,256,512]{2,1,0:T(8,128)} %u_hbm.1, f32[8,256,512]{2,1,0:T(8,128)} %c_hbm.1, f32[4,256,512]{2,1,0:T(8,128)} %cool_hbm.1, s32[256,512]{1,0:T(8,128)} %idx_hbm.1, f32[16]{0:T(128)} %lev_hbm.1, s32[4,512]{1,0:T(4,128)} %mask_hbm.1, f32[4,512]{1,0:T(4,128)} %inlet_hbm.1, ...), custom_call_target="tpu_custom_call" | custom-call | flops 41943040 | bytes 17825792 | tf_op jit(solution)/shard_map/pallas_call | solution.py:413
  33.5 2.0 %copy.12 = f32[8,256,512]{2,1,0:T(8,128)} copy(f32[8,256,512]{2,1,0:T(8,128)S(1)} %get-tuple-element.2) | data formatting | bytes 8388608
  35.5 1.3 %copy.13 = f32[4,256,512]{2,1,0:T(8,128)} copy(f32[4,256,512]{2,1,0:T(8,128)S(1)} %get-tuple-element.3) | data formatting | bytes 4194304
